TPU v7x, 128 devices: a whole 4x4x4 slice. The times are simulated.
128 devices in a mesh: section: 2 (over core), replica: 4 (over y), shard: 16 (over x, z).
Axes of the slice: x: 4, y: 4, z: 4, core: 2. Of those that a mesh axis runs over, the one named last changes fastest.
Arguments:
- inputs: bfloat16 [2, 49152, 512], P(None, ('replica', 'shard')), may hold values from -6 to 6
- cotangent: bfloat16 [2, 49152, 512], P(None, ('replica', 'shard')), may hold values from -6 to 6
- lengths: int32 [2, 64, 4], P(None, ('replica', 'shard')), may hold values from 0 to 768, as said below
- norm1_gain: bfloat16 [2, 512], P('section', 'shard'), may hold values from 0.5 to 1.5
- norm1_bias: bfloat16 [2, 512], P('section', 'shard'), may hold values from -1.5 to 1.5
- qkv_weight: bfloat16 [2, 512, 1536], P('section', 'shard'), may hold values from -0.375 to 0.375
- qkv_bias: bfloat16 [2, 1536], P('section', 'shard'), may hold values from -2.5 to 2.5
- dense_weight: bfloat16 [2, 512, 512], P('section', 'shard'), may hold values from -1 to 1
- norm2_gain: bfloat16 [2, 512], P('section', 'shard'), may hold values from 0.5 to 1.5
- norm2_bias: bfloat16 [2, 512], P('section', 'shard'), may hold values from -1.5 to 1.5
- fc_in_weight: bfloat16 [2, 512, 2048], P('section', 'shard'), may hold values from -0.25 to 0.25
- fc_in_bias: bfloat16 [2, 2048], P('section', 'shard'), may hold values from -2.5 to 2.5
- fc_out_weight: bfloat16 [2, 2048, 512], P('section', 'shard'), may hold values from -0.1875 to 0.1875
- out_bias: bfloat16 [2, 512], P('section', 'shard'), may hold values from -2.5 to 2.5
Outputs:
- activations: bfloat16 [2, 2, 49152, 512], P('section', None, ('replica', 'shard'))
- input_grads: bfloat16 [2, 2, 49152, 512], P('section', None, ('replica', 'shard'))
- grad_norm1_gain: float32 [2, 512], P('section', 'shard')
- grad_norm1_bias: float32 [2, 512], P('section', 'shard')
- grad_qkv_weight: float32 [2, 512, 1536], P('section', 'shard')
- grad_qkv_bias: float32 [2, 1536], P('section', 'shard')
- grad_dense_weight: float32 [2, 512, 512], P('section', 'shard')
- grad_norm2_gain: float32 [2, 512], P('section', 'shard')
- grad_norm2_bias: float32 [2, 512], P('section', 'shard')
- grad_fc_in_weight: float32 [2, 512, 2048], P('section', 'shard')
- grad_fc_in_bias: float32 [2, 2048], P('section', 'shard')
- grad_fc_out_weight: float32 [2, 2048, 512], P('section', 'shard')
- grad_out_bias: float32 [2, 512], P('section', 'shard')
Inputs may be any that keep to these rules, and one draw needn't show every extreme that they name: `lengths`: in each slab the sequences, each padded up to a multiple of 128 rows, fill at most 768 rows; a length of 0 is an empty sequence. In every micro-batch some slab holds a single sequence of 768 rows.
All inputs are finite; a program needn't handle non-finite values.
Results may differ from a plain program's by a relative error of at most 0.025.
Values may be sent and summed in bfloat16 or wider, within the bound.
A program may use at most 256 MiB of HBM per device.

v0:
```python
import math

import jax
import jax.numpy as jnp
from jax import lax
from jax.sharding import PartitionSpec as P

D = 512
HEADS = 8
ROT = 16
HEAD = 64
BLOCK = 128
SEQS = 4
MICRO = 2
TOK_DEV = 768


epsilon = 1e-05
masked_value = -1000000000.0


def passed_along(value, axis, steps):
    count = lax.axis_size(axis)
    initial, last = (max(0, -steps), min(count, count - steps))
    return lax.ppermute(value, axis, [(source, source + steps) for source in range(initial, last)])


def layout(slab_lengths):
    places = jnp.arange(TOK_DEV, dtype=jnp.int32)
    padded = (slab_lengths + BLOCK - 1) // BLOCK * BLOCK
    starts = jnp.cumsum(padded, dtype=jnp.int32) - padded
    inside = (places[:, None] >= starts[None, :]) & (
        places[:, None] < (starts + slab_lengths)[None, :]
    )
    labels = jnp.arange(1, SEQS + 1, dtype=jnp.int32)
    sequence_ids = jnp.sum(jnp.where(inside, labels[None, :], 0), axis=1, dtype=jnp.int32) - 1
    offsets = jnp.sum(
        jnp.where(inside, places[:, None] - starts[None, :], 0), axis=1, dtype=jnp.int32
    )
    alive = sequence_ids >= 0
    allowed = (sequence_ids[:, None] == sequence_ids[None, :]) & (
        places[None, :] <= places[:, None]
    ) & alive[:, None] | (places[:, None] == places[None, :])
    return (alive, offsets, allowed)


def rotary_tables(offsets):
    indices = jnp.arange(ROT // 2, dtype=jnp.float32)
    frequencies = jnp.exp(indices * (-2.0 * math.log(10000.0) / ROT))
    angles = offsets.astype(jnp.float32)[:, None] * frequencies[None, :]
    return (jnp.cos(angles), jnp.sin(angles))


def rotate(by_heads, cosine_table, sine_table, direction):
    half_rot = ROT // 2
    lower_half = by_heads[..., :half_rot]
    upper_half = by_heads[..., half_rot:ROT]
    cosine_part = cosine_table[:, None, :]
    sine_part = sine_table[:, None, :] * direction
    return jnp.concatenate(
        [
            lower_half * cosine_part - upper_half * sine_part,
            upper_half * cosine_part + lower_half * sine_part,
            by_heads[..., ROT:],
        ],
        axis=-1,
    )


def norm_parts(rows_in, gain_row, shift_row):
    average = jnp.mean(rows_in, axis=-1, keepdims=True)
    centred = rows_in - average
    scaled = lax.rsqrt(jnp.mean(centred * centred, axis=-1, keepdims=True) + epsilon)
    unit_rows = centred * scaled
    return (
        unit_rows * gain_row.astype(jnp.float32) + shift_row.astype(jnp.float32),
        unit_rows,
        scaled,
    )


def norm_back(grad_normed, unit_rows, scaled, gain_row):
    weighted = grad_normed * gain_row.astype(jnp.float32)
    centre = jnp.mean(weighted, axis=-1, keepdims=True)
    along = jnp.mean(weighted * unit_rows, axis=-1, keepdims=True)
    return scaled * (weighted - centre - unit_rows * along)


def gelu_slope(values_in):
    return 0.5 * (1.0 + jax.scipy.special.erf(values_in / math.sqrt(2.0))) + values_in * jnp.exp(
        -0.5 * values_in * values_in
    ) / math.sqrt(2.0 * math.pi)


def head_columns(matrix, head_index):
    return lax.dynamic_slice_in_dim(matrix, head_index * HEAD, HEAD, 1)


def join_heads(stacked):
    return jnp.transpose(stacked, (1, 0, 2)).reshape(stacked.shape[1], D)


def run_forward(hidden, slab_lengths, weights):
    (
        gain_one,
        shift_one,
        attend_matrix,
        attend_offset,
        dense_matrix,
        gain_two,
        shift_two,
        widen_matrix,
        widen_offset,
        narrow_matrix,
        output_offset,
    ) = weights
    alive, offsets, allowed = layout(slab_lengths)
    cosine_table, sine_table = rotary_tables(offsets)
    head_scale = 1.0 / math.sqrt(HEAD)
    residual = hidden.astype(jnp.float32)
    normed_one, unit_one, scale_one = norm_parts(residual, gain_one, shift_one)
    normed_one = normed_one.astype(jnp.bfloat16)
    projected = jnp.dot(
        normed_one, attend_matrix, preferred_element_type=jnp.float32
    ) + attend_offset.astype(jnp.float32)
    queries = (
        rotate(projected[:, :D].reshape(TOK_DEV, HEADS, HEAD), cosine_table, sine_table, 1.0)
        .reshape(TOK_DEV, D)
        .astype(jnp.bfloat16)
    )
    keys_all = (
        rotate(projected[:, D : 2 * D].reshape(TOK_DEV, HEADS, HEAD), cosine_table, sine_table, 1.0)
        .reshape(TOK_DEV, D)
        .astype(jnp.bfloat16)
    )
    values_all = projected[:, 2 * D :].astype(jnp.bfloat16)

    def one_head(head_index):
        head_query = head_columns(queries, head_index)
        head_key = head_columns(keys_all, head_index)
        head_value = head_columns(values_all, head_index)
        scores = jnp.where(
            allowed,
            jnp.dot(head_query, head_key.T, preferred_element_type=jnp.float32) * head_scale,
            masked_value,
        )
        row_peak = jnp.max(scores, axis=1, keepdims=True)
        log_total = row_peak + jnp.log(jnp.sum(jnp.exp(scores - row_peak), axis=1, keepdims=True))
        attention = jnp.exp(scores - log_total).astype(jnp.bfloat16)
        return (
            jnp.dot(attention, head_value, preferred_element_type=jnp.float32).astype(jnp.bfloat16),
            log_total[:, 0],
        )

    blended_heads, log_totals = lax.map(one_head, jnp.arange(HEADS, dtype=jnp.int32))
    blended = join_heads(blended_heads)
    attended = jnp.dot(blended, dense_matrix, preferred_element_type=jnp.float32)
    normed_two, unit_two, scale_two = norm_parts(residual, gain_two, shift_two)
    normed_two = normed_two.astype(jnp.bfloat16)
    widened = jnp.dot(
        normed_two, widen_matrix, preferred_element_type=jnp.float32
    ) + widen_offset.astype(jnp.float32)
    activated = jax.nn.gelu(widened, approximate=False).astype(jnp.bfloat16)
    narrowed = jnp.dot(activated, narrow_matrix, preferred_element_type=jnp.float32)
    alive_rows = alive.astype(jnp.float32)[:, None]
    result = (
        (residual + attended + narrowed + output_offset.astype(jnp.float32)) * alive_rows
    ).astype(jnp.bfloat16)
    stored = (
        unit_one,
        scale_one,
        normed_one,
        queries,
        keys_all,
        values_all,
        log_totals,
        blended,
        unit_two,
        scale_two,
        normed_two,
        widened,
    )
    return (result, stored)


def skip_forward(hidden, slab_lengths, weights):
    return jax.tree.map(jnp.zeros_like, run_forward(hidden, slab_lengths, weights))


def run_backward(upstream, stored, slab_lengths, weights):
    (
        gain_one,
        shift_one,
        attend_matrix,
        attend_offset,
        dense_matrix,
        gain_two,
        shift_two,
        widen_matrix,
        widen_offset,
        narrow_matrix,
        output_offset,
    ) = weights
    (
        unit_one,
        scale_one,
        normed_one,
        queries,
        keys_all,
        values_all,
        log_totals,
        blended,
        unit_two,
        scale_two,
        normed_two,
        widened,
    ) = stored
    alive, offsets, allowed = layout(slab_lengths)
    cosine_table, sine_table = rotary_tables(offsets)
    head_scale = 1.0 / math.sqrt(HEAD)
    carried = upstream.astype(jnp.float32) * alive.astype(jnp.float32)[:, None]
    carried_low = carried.astype(jnp.bfloat16)
    grad_output_offset = jnp.sum(carried, axis=0)
    activated = jax.nn.gelu(widened, approximate=False).astype(jnp.bfloat16)
    grad_narrow_matrix = jnp.dot(activated.T, carried_low, preferred_element_type=jnp.float32)
    grad_activated = jnp.dot(carried_low, narrow_matrix.T, preferred_element_type=jnp.float32)
    grad_widened = (grad_activated * gelu_slope(widened)).astype(jnp.bfloat16)
    grad_widen_offset = jnp.sum(grad_widened.astype(jnp.float32), axis=0)
    grad_widen_matrix = jnp.dot(normed_two.T, grad_widened, preferred_element_type=jnp.float32)
    grad_normed_two = jnp.dot(grad_widened, widen_matrix.T, preferred_element_type=jnp.float32)
    grad_gain_two = jnp.sum(grad_normed_two * unit_two, axis=0)
    grad_shift_two = jnp.sum(grad_normed_two, axis=0)
    grad_dense_matrix = jnp.dot(blended.T, carried_low, preferred_element_type=jnp.float32)
    grad_blended = jnp.dot(carried_low, dense_matrix.T, preferred_element_type=jnp.float32).astype(
        jnp.bfloat16
    )

    def one_head(head_index):
        head_query = head_columns(queries, head_index)
        head_key = head_columns(keys_all, head_index)
        head_value = head_columns(values_all, head_index)
        head_grad = head_columns(grad_blended, head_index)
        log_total = lax.dynamic_index_in_dim(log_totals, head_index, 0, False)
        scores = jnp.where(
            allowed,
            jnp.dot(head_query, head_key.T, preferred_element_type=jnp.float32) * head_scale,
            masked_value,
        )
        full_probs = jnp.exp(scores - log_total[:, None])
        grad_value = jnp.dot(
            full_probs.astype(jnp.bfloat16).T, head_grad, preferred_element_type=jnp.float32
        )
        grad_probs = jnp.dot(head_grad, head_value.T, preferred_element_type=jnp.float32)
        centre = jnp.sum(full_probs * grad_probs, axis=1, keepdims=True)
        grad_scores = (full_probs * (grad_probs - centre)).astype(jnp.bfloat16)
        grad_query = jnp.dot(grad_scores, head_key, preferred_element_type=jnp.float32) * head_scale
        grad_key = (
            jnp.dot(grad_scores.T, head_query, preferred_element_type=jnp.float32) * head_scale
        )
        return (grad_query, grad_key, grad_value)

    grad_queries, grad_keys, grad_values = lax.map(one_head, jnp.arange(HEADS, dtype=jnp.int32))
    grad_queries = rotate(
        jnp.transpose(grad_queries, (1, 0, 2)), cosine_table, sine_table, -1.0
    ).reshape(TOK_DEV, D)
    grad_keys = rotate(jnp.transpose(grad_keys, (1, 0, 2)), cosine_table, sine_table, -1.0).reshape(
        TOK_DEV, D
    )
    grad_projected = jnp.concatenate(
        [grad_queries, grad_keys, join_heads(grad_values)], axis=1
    ).astype(jnp.bfloat16)
    grad_attend_offset = jnp.sum(grad_projected.astype(jnp.float32), axis=0)
    grad_attend_matrix = jnp.dot(normed_one.T, grad_projected, preferred_element_type=jnp.float32)
    grad_normed_one = jnp.dot(grad_projected, attend_matrix.T, preferred_element_type=jnp.float32)
    grad_gain_one = jnp.sum(grad_normed_one * unit_one, axis=0)
    grad_shift_one = jnp.sum(grad_normed_one, axis=0)
    grad_residual = (
        carried
        + norm_back(grad_normed_one, unit_one, scale_one, gain_one)
        + norm_back(grad_normed_two, unit_two, scale_two, gain_two)
    )
    gradients = (
        grad_gain_one,
        grad_shift_one,
        grad_attend_matrix,
        grad_attend_offset,
        grad_dense_matrix,
        grad_gain_two,
        grad_shift_two,
        grad_widen_matrix,
        grad_widen_offset,
        grad_narrow_matrix,
        grad_output_offset,
    )
    return (grad_residual.astype(jnp.bfloat16), gradients)


def skip_backward(upstream, stored, slab_lengths, weights):
    return jax.tree.map(jnp.zeros_like, run_backward(upstream, stored, slab_lengths, weights))


def body(
    inputs,
    cotangent,
    lengths,
    norm1_gain,
    norm1_bias,
    qkv_weight,
    qkv_bias,
    dense_weight,
    norm2_gain,
    norm2_bias,
    fc_in_weight,
    fc_in_bias,
    fc_out_weight,
    out_bias,
):
    leading = lax.axis_index("section") == 0
    trailing = jnp.logical_not(leading)
    zero_rows = jnp.zeros(inputs.shape[1:], jnp.bfloat16)

    def fetch_forward():
        members = (
            lax.all_gather(norm1_gain, "shard", axis=1, tiled=True),
            lax.all_gather(norm1_bias, "shard", axis=1, tiled=True),
            lax.all_gather(qkv_weight, "shard", axis=1, tiled=True),
            lax.all_gather(qkv_bias, "shard", axis=1, tiled=True),
            lax.all_gather(dense_weight, "shard", axis=1, tiled=True),
            lax.all_gather(norm2_gain, "shard", axis=1, tiled=True),
            lax.all_gather(norm2_bias, "shard", axis=1, tiled=True),
            lax.all_gather(fc_in_weight, "shard", axis=1, tiled=True),
            lax.all_gather(fc_in_bias, "shard", axis=1, tiled=True),
            lax.all_gather(fc_out_weight, "shard", axis=1, tiled=True),
            lax.all_gather(out_bias, "shard", axis=1, tiled=True),
        )
        return tuple((member[0] for member in members))

    def fetch_backward():
        members = (
            lax.all_gather(norm1_gain, "shard", axis=1, tiled=True),
            lax.all_gather(norm1_bias, "shard", axis=1, tiled=True),
            lax.all_gather(qkv_weight, "shard", axis=1, tiled=True),
            lax.all_gather(qkv_bias, "shard", axis=1, tiled=True),
            lax.all_gather(dense_weight, "shard", axis=1, tiled=True),
            lax.all_gather(norm2_gain, "shard", axis=1, tiled=True),
            lax.all_gather(norm2_bias, "shard", axis=1, tiled=True),
            lax.all_gather(fc_in_weight, "shard", axis=1, tiled=True),
            lax.all_gather(fc_in_bias, "shard", axis=1, tiled=True),
            lax.all_gather(fc_out_weight, "shard", axis=1, tiled=True),
            lax.all_gather(out_bias, "shard", axis=1, tiled=True),
        )
        return tuple((member[0] for member in members))

    received = zero_rows
    results = []
    stores = []
    for moment in range(MICRO + 1):
        weights = fetch_forward()
        own_input = inputs[min(moment, MICRO - 1)]
        hidden = jnp.where(leading, own_input, received)
        slab_lengths = jnp.where(
            leading, lengths[min(moment, MICRO - 1), 0], lengths[max(moment - 1, 0), 0]
        )
        if moment == 0 or moment == MICRO:
            active = leading if moment == 0 else trailing
            output, stored = lax.cond(
                active, run_forward, skip_forward, hidden, slab_lengths, weights
            )
        else:
            output, stored = run_forward(hidden, slab_lengths, weights)
        results.append(output)
        stores.append(stored)
        if moment < MICRO:
            received = passed_along(output, "section", 1)
    activations = jnp.stack(
        [
            jnp.where(leading, results[index_micro], results[index_micro + 1])
            for index_micro in range(MICRO)
        ]
    )[None]
    returned = zero_rows
    handed_back = []
    totals = None
    for moment in range(MICRO + 1):
        weights = fetch_backward()
        upstream = jnp.where(leading, returned, cotangent[min(moment, MICRO - 1)])
        stored = jax.tree.map(
            lambda from_before, from_after: jnp.where(leading, from_before, from_after),
            stores[max(moment - 1, 0)],
            stores[min(moment + 1, MICRO)],
        )
        slab_lengths = jnp.where(
            leading, lengths[max(moment - 1, 0), 0], lengths[min(moment, MICRO - 1), 0]
        )
        if moment == 0 or moment == MICRO:
            active = trailing if moment == 0 else leading
            grad_hidden, gradients = lax.cond(
                active, run_backward, skip_backward, upstream, stored, slab_lengths, weights
            )
        else:
            grad_hidden, gradients = run_backward(upstream, stored, slab_lengths, weights)
        handed_back.append(grad_hidden)
        if moment < MICRO:
            returned = passed_along(grad_hidden, "section", -1)
        (
            grad_gain_one,
            grad_shift_one,
            grad_attend_matrix,
            grad_attend_offset,
            grad_dense_matrix,
            grad_gain_two,
            grad_shift_two,
            grad_widen_matrix,
            grad_widen_offset,
            grad_narrow_matrix,
            grad_output_offset,
        ) = gradients
        shares = (
            lax.psum_scatter(
                grad_gain_one.astype(jnp.bfloat16), "shard", scatter_dimension=0, tiled=True
            ).astype(jnp.float32),
            lax.psum_scatter(
                grad_shift_one.astype(jnp.bfloat16), "shard", scatter_dimension=0, tiled=True
            ).astype(jnp.float32),
            lax.psum_scatter(
                grad_attend_matrix.astype(jnp.bfloat16), "shard", scatter_dimension=0, tiled=True
            ).astype(jnp.float32),
            lax.psum_scatter(
                grad_attend_offset.astype(jnp.bfloat16), "shard", scatter_dimension=0, tiled=True
            ).astype(jnp.float32),
            lax.psum_scatter(
                grad_dense_matrix.astype(jnp.bfloat16), "shard", scatter_dimension=0, tiled=True
            ).astype(jnp.float32),
            lax.psum_scatter(
                grad_gain_two.astype(jnp.bfloat16), "shard", scatter_dimension=0, tiled=True
            ).astype(jnp.float32),
            lax.psum_scatter(
                grad_shift_two.astype(jnp.bfloat16), "shard", scatter_dimension=0, tiled=True
            ).astype(jnp.float32),
            lax.psum_scatter(
                grad_widen_matrix.astype(jnp.bfloat16), "shard", scatter_dimension=0, tiled=True
            ).astype(jnp.float32),
            lax.psum_scatter(
                grad_widen_offset.astype(jnp.bfloat16), "shard", scatter_dimension=0, tiled=True
            ).astype(jnp.float32),
            lax.psum_scatter(
                grad_narrow_matrix.astype(jnp.bfloat16), "shard", scatter_dimension=0, tiled=True
            ).astype(jnp.float32),
            lax.psum_scatter(
                grad_output_offset.astype(jnp.bfloat16), "shard", scatter_dimension=0, tiled=True
            ).astype(jnp.float32),
        )
        (
            share_gain_one,
            share_shift_one,
            share_attend_matrix,
            share_attend_offset,
            share_dense_matrix,
            share_gain_two,
            share_shift_two,
            share_widen_matrix,
            share_widen_offset,
            share_narrow_matrix,
            share_output_offset,
        ) = shares
        summed = (
            lax.psum(share_gain_one.astype(jnp.bfloat16), "replica").astype(jnp.float32),
            lax.psum(share_shift_one.astype(jnp.bfloat16), "replica").astype(jnp.float32),
            lax.psum(share_attend_matrix.astype(jnp.bfloat16), "replica").astype(jnp.float32),
            lax.psum(share_attend_offset.astype(jnp.bfloat16), "replica").astype(jnp.float32),
            lax.psum(share_dense_matrix.astype(jnp.bfloat16), "replica").astype(jnp.float32),
            lax.psum(share_gain_two.astype(jnp.bfloat16), "replica").astype(jnp.float32),
            lax.psum(share_shift_two.astype(jnp.bfloat16), "replica").astype(jnp.float32),
            lax.psum(share_widen_matrix.astype(jnp.bfloat16), "replica").astype(jnp.float32),
            lax.psum(share_widen_offset.astype(jnp.bfloat16), "replica").astype(jnp.float32),
            lax.psum(share_narrow_matrix.astype(jnp.bfloat16), "replica").astype(jnp.float32),
            lax.psum(share_output_offset.astype(jnp.bfloat16), "replica").astype(jnp.float32),
        )
        totals = (
            tuple(summed)
            if totals is None
            else tuple((before + after for before, after in zip(totals, summed)))
        )
    input_grads = jnp.stack(
        [
            jnp.where(leading, handed_back[index_micro + 1], handed_back[index_micro])
            for index_micro in range(MICRO)
        ]
    )[None]
    (
        total_gain_one,
        total_shift_one,
        total_attend_matrix,
        total_attend_offset,
        total_dense_matrix,
        total_gain_two,
        total_shift_two,
        total_widen_matrix,
        total_widen_offset,
        total_narrow_matrix,
        total_output_offset,
    ) = totals
    return (
        activations,
        input_grads,
        total_gain_one[None],
        total_shift_one[None],
        total_attend_matrix[None],
        total_attend_offset[None],
        total_dense_matrix[None],
        total_gain_two[None],
        total_shift_two[None],
        total_widen_matrix[None],
        total_widen_offset[None],
        total_narrow_matrix[None],
        total_output_offset[None],
    )


def solution(mesh):
    placed = (
        P(None, ("replica", "shard"), None),
        P(None, ("replica", "shard"), None),
        P(None, ("replica", "shard"), None),
        P("section", "shard"),
        P("section", "shard"),
        P("section", "shard", None),
        P("section", "shard"),
        P("section", "shard", None),
        P("section", "shard"),
        P("section", "shard"),
        P("section", "shard", None),
        P("section", "shard"),
        P("section", "shard", None),
        P("section", "shard"),
    )
    return jax.shard_map(
        body,
        mesh=mesh,
        in_specs=placed,
        out_specs=(
            P("section", None, ("replica", "shard"), None),
            P("section", None, ("replica", "shard"), None),
            P("section", "shard"),
            P("section", "shard"),
            P("section", "shard", None),
            P("section", "shard"),
            P("section", "shard", None),
            P("section", "shard"),
            P("section", "shard"),
            P("section", "shard", None),
            P("section", "shard"),
            P("section", "shard", None),
            P("section", "shard"),
        ),
        check_vma=False,
    )
```

profile of v0, /device:TPU:0, one launch (start us, length us, event | category | flops | bytes accessed | tf_op | source)
XLA Modules:
  0.0 1878.4 jit_solution(2324167673011543120)
XLA Ops:
  17.2 43.0 %all-reduce.28 = (bf16[512]{0:T(512)(128)(2,1)S(1)}, bf16[512]{0:T(512)(128)(2,1)S(1)}, bf16[512]{0:T(512)(128)(2,1)S(1)}, bf16[512]{0:T(512)(128)(2,1)S(1)}, bf...) all-reduce(bf16[512]{0:T(512)(128)(2,1)S(1)} %dynamic-update-slice., ...), channel_id=1, replica_groups=mesh['section'=2,'replica'=4,'shard'=16] {'shard'}, use_global_device_ids=true, to_apply=%add.4 | all-reduce | flops 4096 | bytes 16384 | tf_op jit(solution)/shard_map/squeeze | solution.py:336
  62.5 17.0 all_gather.30
  84.9 26.1 %all_gather.26 = bf16[1,512,512]{2,1,0:T(8,128)(2,1)} all-gather(bf16[1,32,512]{2,1,0:T(8,128)(2,1)} %param.41), channel_id=1, replica_groups=mesh['section'=2,'replica'=4,'shard'=16] {'shard'}, dimensions={1}, use_global_device_ids=true | all-gather | bytes 557056 | tf_op jit(solution)/shard_map/all_gather | solution.py:328
  112.2 38.1 %all-gather.8.cloned.1.call-done = bf16[1,2048,512]{2,1,0:T(8,128)(2,1)} async-done(((bf16[1,128,512]{2,1,0:T(8,128)(2,1)}), bf16[1,2048,512]{2,1,0:T(8,128)(2,1)}) %all-gather.8.cloned.1.call-update) | async-done | bytes 2097168 | tf_op jit(solution)/shard_map/all_gather | solution.py:333
  151.3 106.7 %conditional.4 = (bf16[768,512]{1,0:T(8,128)(2,1)}, f32[768,512]{1,0:T(8,128)}, f32[768,1]{0,1:T(1,128)S(1)}, bf16[768,512]{1,0:T(8,128)(2,1)}, bf16[768,512]{0,...) conditional(s32[]{:T(128)} %convert_element_type.635, () %tuple.72, ...), branch_computations={%region_0.1_spmd, %region_1.11_spmd} | conditional | flops 5109732864 | bytes 129548152 | solution.py:366
  154.7 2.8 add_convert_fusion
  157.5 5.7 convolution_add_fusion.1
  163.2 16.5 fusion.35
  183.8 3.0 copy.119
  197.9 54.3 %while.88 = (s32[]{:T(128)}, bf16[8,768,64]{1,2,0:T(8,128)(2,1)}, f32[8,768]{1,0:T(8,128)}, s32[8]{0:T(128)S(1)}, bf16[768,512]{1,0:T(8,128)(2,1)}, /*index=5*/b...) while((s32[]{:T(128)}, bf16[8,768,64]{1,2,0:T(8,128)(2,1)}, ...), condition=%wide.region_10.10_spmd.clone, body=%wide.region_7.9_spmd.clone.sunk | while | flops 158711040 | bytes 7810251 | solution.py:155
  252.2 3.3 fusion.43
  269.2 3.0 copy.127
  278.9 39.5 %while.92 = (s32[]{:T(128)}, bf16[8,768,64]{1,2,0:T(8,128)(2,1)}, f32[8,768]{1,0:T(8,128)}, s32[8]{0:T(128)S(1)}, bf16[768,512]{0,1:T(8,128)(2,1)S(1)}, /*index=...) while((s32[]{:T(128)}, bf16[8,768,64]{1,2,0:T(8,128)(2,1)}, ...), condition=%wide.region_19.20_spmd.clone, body=%wide.region_16.19_spmd.clone.sunk | while | flops 158711040 | bytes 7614667 | solution.py:155
  318.5 4.2 convolution_add_fusion.5
  322.8 13.7 fusion.396
  338.0 3.4 collective-permute-start.1
  344.4 14.0 conditional.6
  362.8 23.2 %conditional.5 = (bf16[768,512]{1,0:T(8,128)(2,1)}, f32[768,512]{1,0:T(8,128)}, f32[768,1]{0,1:T(1,128)S(1)}, bf16[768,512]{1,0:T(8,128)(2,1)}, bf16[768,512]{0,...) conditional(s32[]{:T(128)} %convert_element_type.645, () %tuple.75, ...), branch_computations={%region_20.21_spmd, %region_21.31_spmd} | conditional | flops 5109732864 | bytes 123297736 | solution.py:366
  371.4 3.4 broadcast.1548
  387.5 150.1 %collective-permute-done.2 = bf16[768,512]{1,0:T(8,128)(2,1)} collective-permute-done((bf16[768,512]{1,0:T(8,128)(2,1)}, bf16[768,512]{1,0:T(8,128)(2,1)}, u32[]{:S(2)}, u32[]{:S(2)}) %collective-permute-start.2) | collective-permute-done | bytes 786464 | tf_op jit(solution)/shard_map/ppermute | solution.py:25
  546.3 114.6 %while.93 = (s32[]{:T(128)}, f32[8,768,64]{1,2,0:T(8,128)}, f32[8,768,64]{1,2,0:T(8,128)}, bf16[8,768,64]{1,2,0:T(8,128)(2,1)}, s32[8]{0:T(128)S(1)}, /*index=5*...) while((s32[]{:T(128)}, f32[8,768,64]{1,2,0:T(8,128)}, ...), condition=%wide.region_54.55_spmd.clone, body=%wide.region_52.54_spmd.clone.sunk | while | flops 386432256 | bytes 19689044 | solution.py:262
  665.8 6.6 fusion.524
  675.6 6.0 multiply_reduce_fusion.15
  687.4 4.1 select_bitcast_fusion.1
  693.7 121.3 %collective-permute-done.3 = bf16[768,512]{1,0:T(8,128)(2,1)} collective-permute-done((bf16[768,512]{1,0:T(8,128)(2,1)S(1)}, bf16[768,512]{1,0:T(8,128)(2,1)}, u32[]{:S(2)}, u32[]{:S(2)}) %collective-permute-start.3) | collective-permute-done | bytes 786464 | tf_op jit(solution)/shard_map/ppermute | solution.py:25
  815.1 179.1 %conditional.7 = (bf16[768,512]{1,0:T(8,128)(2,1)}, bf16[512]{0:T(512)(128)(2,1)}, bf16[512]{0:T(512)(128)(2,1)}, bf16[512,1536]{1,0:T(8,128)(2,1)}, bf16[1536]{...) conditional(s32[]{:T(128)} %convert_element_type.635, () %tuple.80, ...), branch_computations={%region_60.61_spmd, %region_61.79_spmd} | conditional | flops 10223165440 | bytes 243104448 | solution.py:397
  821.4 3.3 fusion.521
  830.4 106.4 %while.91 = (s32[]{:T(128)}, f32[8,768,64]{1,2,0:T(8,128)}, f32[8,768,64]{1,2,0:T(8,128)}, bf16[8,768,64]{1,2,0:T(8,128)(2,1)}, s32[8]{0:T(128)S(1)}, /*index=5*...) while((s32[]{:T(128)}, f32[8,768,64]{1,2,0:T(8,128)}, ...), condition=%wide.region_66.66_spmd.clone, body=%wide.region_64.65_spmd.clone.sunk | while | flops 386432256 | bytes 19701212 | solution.py:262
  945.8 7.3 convert_reduce_fusion.4
  953.2 5.8 multiply_reduce_fusion.8
  967.4 2.8 fusion.297
  970.2 5.3 fusion.295
  975.4 18.5 fusion.290
  998.6 73.0 %all-reduce.27 = (bf16[512]{0:T(512)(128)(2,1)S(1)}, bf16[512]{0:T(512)(128)(2,1)S(1)}, bf16[512]{0:T(512)(128)(2,1)S(1)}, bf16[512]{0:T(512)(128)(2,1)S(1)}, bf...) all-reduce(bf16[512]{0:T(512)(128)(2,1)} %get-tuple-element.802, ...), channel_id=4, replica_groups=mesh['section'=2,'replica'=4,'shard'=16] {'shard'}, use_global_device_ids=true, to_apply=%region_84.85.clone | all-reduce | flops 18432 | bytes 73728
  1085.3 3.8 convolution_convert_fusion.3
  1091.1 5.3 convolution_convert_fusion.2
  1096.5 17.7 fusion.398
  1120.7 3.5 all-reduce.34.cloned.1.call-done
  1127.8 74.5 %reduce-scatter.13.cloned.1.call-done = bf16[32,1536]{1,0:T(8,128)(2,1)} async-done(((bf16[512,1536]{1,0:T(8,128)(2,1)}), bf16[32,1536]{1,0:T(8,128)(2,1)}) %reduce-scatter.13.cloned.1.call-update) | async-done | bytes 98320 | tf_op jit(solution)/shard_map/reduce_scatter | solution.py:425
  1202.3 76.3 %reduce-scatter.15.cloned.1.call-done = bf16[32,1536]{1,0:T(8,128)(2,1)} async-done(((bf16[512,1536]{1,0:T(8,128)(2,1)}), bf16[32,1536]{1,0:T(8,128)(2,1)}) %reduce-scatter.15.cloned.1.call-update) | async-done | bytes 98320 | tf_op jit(solution)/shard_map/reduce_scatter | solution.py:425
  1278.6 76.9 %reduce-scatter.25.cloned.1.call-done = bf16[32,2048]{1,0:T(8,128)(2,1)} async-done(((bf16[512,2048]{1,0:T(8,128)(2,1)}), bf16[32,2048]{1,0:T(8,128)(2,1)}) %reduce-scatter.25.cloned.1.call-update) | async-done | bytes 131088 | tf_op jit(solution)/shard_map/reduce_scatter | solution.py:440
  1355.5 77.3 %reduce-scatter.31.cloned.1.call-done = bf16[128,512]{1,0:T(8,128)(2,1)} async-done(((bf16[2048,512]{1,0:T(8,128)(2,1)}), bf16[128,512]{1,0:T(8,128)(2,1)}) %reduce-scatter.31.cloned.1.call-update) | async-done | bytes 131088 | tf_op jit(solution)/shard_map/reduce_scatter | solution.py:446
  1432.8 76.0 %reduce-scatter.17.cloned.1.call-done = bf16[32,1536]{1,0:T(8,128)(2,1)} async-done(((bf16[512,1536]{1,0:T(8,128)(2,1)}), bf16[32,1536]{1,0:T(8,128)(2,1)}) %reduce-scatter.17.cloned.1.call-update) | async-done | bytes 98320 | tf_op jit(solution)/shard_map/reduce_scatter | solution.py:425
  1508.8 77.1 %reduce-scatter.27.cloned.1.call-done = bf16[32,2048]{1,0:T(8,128)(2,1)} async-done(((bf16[512,2048]{1,0:T(8,128)(2,1)}), bf16[32,2048]{1,0:T(8,128)(2,1)}) %reduce-scatter.27.cloned.1.call-update) | async-done | bytes 131088 | tf_op jit(solution)/shard_map/reduce_scatter | solution.py:440
  1586.0 77.3 %reduce-scatter.33.cloned.1.call-done = bf16[128,512]{1,0:T(8,128)(2,1)} async-done(((bf16[2048,512]{1,0:T(8,128)(2,1)}), bf16[128,512]{1,0:T(8,128)(2,1)}) %reduce-scatter.33.cloned.1.call-update) | async-done | bytes 131088 | tf_op jit(solution)/shard_map/reduce_scatter | solution.py:446
  1663.2 76.8 %reduce-scatter.29.cloned.1.call-done = bf16[32,2048]{1,0:T(8,128)(2,1)} async-done(((bf16[512,2048]{1,0:T(8,128)(2,1)}), bf16[32,2048]{1,0:T(8,128)(2,1)}) %reduce-scatter.29.cloned.1.call-update) | async-done | bytes 131088 | tf_op jit(solution)/shard_map/reduce_scatter | solution.py:440
  1740.0 77.2 %reduce-scatter.35.cloned.1.call-done = bf16[128,512]{1,0:T(8,128)(2,1)} async-done(((bf16[2048,512]{1,0:T(8,128)(2,1)}), bf16[128,512]{1,0:T(8,128)(2,1)}) %reduce-scatter.35.cloned.1.call-update) | async-done | bytes 131088 | tf_op jit(solution)/shard_map/reduce_scatter | solution.py:446
  1823.4 42.8 %all-reduce.36.cloned.1.call-done = (bf16[32,1536]{1,0:T(8,128)(2,1)}, bf16[32,1536]{1,0:T(8,128)(2,1)}, bf16[32,1536]{1,0:T(8,128)(2,1)}, bf16[32,2048]{1,0:T(8...) async-done(((bf16[32,1536]{1,0:T(8,128)(2,1)}, ...) | async-done | bytes 1081360 | tf_op jit(solution)/shard_map/psum | solution.py:469
  (780 shorter events, 444.0 us)
Async XLA Ops:
  7.2 105.1 %all-gather.4.cloned.1.call-start = ((), (), s32[]{:S(2)}) async-start(), calls=%async_computation.12 | async-start | bytes 1671168 | tf_op jit(solution)/shard_map/all_gather | solution.py:326
  7.9 104.3 %all-gather.6.cloned.1.call-start = ((), (), s32[]{:S(2)}) async-start(), calls=%async_computation.13 | async-start | bytes 2228224 | tf_op jit(solution)/shard_map/all_gather | solution.py:331
  8.7 141.7 %all-gather.8.cloned.1.call-start = ((), (), s32[]{:S(2)}) async-start(), calls=%async_computation.14 | async-start | bytes 2228224 | tf_op jit(solution)/shard_map/all_gather | solution.py:333
  9.4 1075.0 %reduce-scatter.19.cloned.1.call-start = ((), (), s32[]{:S(2)}) async-start(), calls=%async_computation.18 | async-start | bytes 557056 | tf_op jit(solution)/shard_map/reduce_scatter | solution.py:431
  60.3 90.2 %copy-start.80 = (bf16[1536]{0:T(1024)(128)(2,1)}, bf16[1536]{0:T(1024)(128)(2,1)S(1)}, u32[]{:S(2)}) copy-start(bf16[1536]{0:T(1024)(128)(2,1)S(1)} %get-tuple-element.1610) | copy-start | bytes 9220
  60.3 90.2 %copy-start.94 = (bf16[512]{0:T(512)(128)(2,1)}, bf16[512]{0:T(512)(128)(2,1)S(1)}, u32[]{:S(2)}) copy-start(bf16[512]{0:T(512)(128)(2,1)S(1)} %get-tuple-element.1607) | copy-start | bytes 3076
  60.3 90.2 %copy-start.97 = (bf16[512]{0:T(512)(128)(2,1)}, bf16[512]{0:T(512)(128)(2,1)S(1)}, u32[]{:S(2)}) copy-start(bf16[512]{0:T(512)(128)(2,1)S(1)} %get-tuple-element.1608) | copy-start | bytes 3076
  60.3 90.2 %copy-start.105 = (bf16[512]{0:T(512)(128)(2,1)}, bf16[512]{0:T(512)(128)(2,1)S(1)}, u32[]{:S(2)}) copy-start(bf16[512]{0:T(512)(128)(2,1)S(1)} %get-tuple-element.1606) | copy-start | bytes 3076
  60.3 90.2 %copy-start.107 = (bf16[512]{0:T(512)(128)(2,1)}, bf16[512]{0:T(512)(128)(2,1)S(1)}, u32[]{:S(2)}) copy-start(bf16[512]{0:T(512)(128)(2,1)S(1)} %get-tuple-element.1609) | copy-start | bytes 3076
  60.3 90.2 %copy-start.108 = (bf16[512]{0:T(512)(128)(2,1)}, bf16[512]{0:T(512)(128)(2,1)S(1)}, u32[]{:S(2)}) copy-start(bf16[512]{0:T(512)(128)(2,1)S(1)} %get-tuple-element.1611) | copy-start | bytes 3076
  79.5 71.0 %copy-start.76 = (bf16[2048]{0:T(1024)(128)(2,1)}, bf16[2048]{0:T(1024)(128)(2,1)S(1)}, u32[]{:S(2)}) copy-start(bf16[2048]{0:T(1024)(128)(2,1)S(1)} %reduce.7) | copy-start | bytes 12292
  154.7 25.0 %copy-start.54 = (bf16[768,512]{1,0:T(8,128)(2,1)}, bf16[768,512]{1,0:T(8,128)(2,1)S(1)}, u32[]{:S(2)}) copy-start(bf16[768,512]{1,0:T(8,128)(2,1)S(1)} %get-tuple-element.2397) | copy-start | bytes 2359300 | tf_op jit(solution)/shard_map/cond
  163.2 16.5 copy-start.144
  197.9 54.3 %copy-start.110 = (bf16[512]{0:T(512)(128)(2,1)S(1)}, bf16[512]{0:T(512)(128)(2,1)}, u32[]{:S(2)}) copy-start(bf16[512]{0:T(512)(128)(2,1)} %copy-done.109) | copy-start | bytes 3076 | tf_op jit(solution)/shard_map/cond
  197.9 54.3 %copy-start.68 = (bf16[512,512]{1,0:T(8,128)(2,1)S(1)}, bf16[512,512]{1,0:T(8,128)(2,1)}, u32[]{:S(2)}) copy-start(bf16[512,512]{1,0:T(8,128)(2,1)} %get-tuple-element.557) | copy-start | bytes 1572868 | tf_op jit(solution)/shard_map/cond
  258.1 3.4 collective-permute-start
  278.9 39.6 %copy-start.116 = (f32[2048]{0:T(1024)S(1)}, f32[2048]{0:T(1024)}, u32[]{:S(2)}) copy-start(f32[2048]{0:T(1024)} %add.895) | copy-start | bytes 24580
  318.4 25.9 %copy-start = (bf16[768,512]{0,1:T(8,128)(2,1)}, bf16[768,512]{0,1:T(8,128)(2,1)S(1)}, u32[]{:S(2)}) copy-start(bf16[768,512]{0,1:T(8,128)(2,1)S(1)} %get-tuple-element.2658) | copy-start | bytes 2359300
  318.4 25.9 %copy-start.2 = (bf16[768,512]{0,1:T(8,128)(2,1)}, bf16[768,512]{0,1:T(8,128)(2,1)S(1)}, u32[]{:S(2)}) copy-start(bf16[768,512]{0,1:T(8,128)(2,1)S(1)} %get-tuple-element.2659) | copy-start | bytes 2359300
  338.0 24.8 %collective-permute-start.1 = (bf16[768,512]{1,0:T(8,128)(2,1)}, bf16[768,512]{1,0:T(8,128)(2,1)}, u32[]{:S(2)}, u32[]{:S(2)}) collective-permute-start(bf16[768,512]{1,0:T(8,128)(2,1)} %fusion.407), channel_id=1, source_target_pairs={{0,64},{1,65},{2,66},{3,67},{4,68},{5,69},{6,70},{7,71},{8,72},{9,... | collective-permute-start | bytes 2359304 | tf_op jit(solution)/shard_map/ppermute | solution.py:25
  344.4 15.3 copy-start.82
  344.4 18.5 copy-start.77
  358.4 179.2 %collective-permute-start.2 = (bf16[768,512]{1,0:T(8,128)(2,1)}, bf16[768,512]{1,0:T(8,128)(2,1)}, u32[]{:S(2)}, u32[]{:S(2)}) collective-permute-start(bf16[768,512]{1,0:T(8,128)(2,1)} %get-tuple-element.786), channel_id=1, source_target_pairs={{64,0},{65,1},{66,2},{67,3},{68,4},{69,5},{70,6},{71,7},{72,8},{73... | collective-permute-start | bytes 2359304 | tf_op jit(solution)/shard_map/ppermute | solution.py:25
  362.8 721.6 %reduce-scatter.21.cloned.1.call-start = ((), (), s32[]{:S(2)}) async-start(), calls=%async_computation.19 | async-start | bytes 557056 | tf_op jit(solution)/shard_map/reduce_scatter | solution.py:431
  386.1 155.4 %copy-start.88 = (f32[768,1]{0,1:T(1,128)}, f32[768,1]{0,1:T(1,128)S(1)}, u32[]{:S(2)}) copy-start(f32[768,1]{0,1:T(1,128)S(1)} %get-tuple-element.787) | copy-start | bytes 9220
  386.1 153.8 %copy-start.67 = (bf16[1,512,512]{2,1,0:T(8,128)(2,1)S(1)}, bf16[1,512,512]{2,1,0:T(8,128)(2,1)}, u32[]{:S(2)}) copy-start(bf16[1,512,512]{2,1,0:T(8,128)(2,1)} %all_gather.26) | copy-start | bytes 1572868
  687.3 397.1 %reduce-scatter.23.cloned.1.call-start = ((), (), s32[]{:S(2)}) async-start(), calls=%async_computation.20 | async-start | bytes 557056 | tf_op jit(solution)/shard_map/reduce_scatter | solution.py:431
  687.4 127.7 %copy-start.1 = (bf16[768,512]{0,1:T(8,128)(2,1)S(1)}, bf16[768,512]{0,1:T(8,128)(2,1)}, u32[]{:S(2)}) copy-start(bf16[768,512]{0,1:T(8,128)(2,1)} %copy-done) | copy-start | bytes 2359300
  687.4 127.7 %copy-start.3 = (bf16[768,512]{0,1:T(8,128)(2,1)S(1)}, bf16[768,512]{0,1:T(8,128)(2,1)}, u32[]{:S(2)}) copy-start(bf16[768,512]{0,1:T(8,128)(2,1)} %copy-done.2) | copy-start | bytes 2359300
  687.4 127.7 %copy-start.8 = (bf16[768,512]{0,1:T(8,128)(2,1)S(1)}, bf16[768,512]{0,1:T(8,128)(2,1)}, u32[]{:S(2)}) copy-start(bf16[768,512]{0,1:T(8,128)(2,1)} %get-tuple-element.788) | copy-start | bytes 2359300
  687.4 127.7 %copy-start.95 = (bf16[512]{0:T(512)(128)(2,1)S(1)}, bf16[512]{0:T(512)(128)(2,1)}, u32[]{:S(2)}) copy-start(bf16[512]{0:T(512)(128)(2,1)} %copy-done.94) | copy-start | bytes 3076
  691.5 123.6 %copy-start.26 = (bf16[768,512]{1,0:T(8,128)(2,1)}, bf16[768,512]{1,0:T(8,128)(2,1)S(1)}, u32[]{:S(2)}) copy-start(bf16[768,512]{1,0:T(8,128)(2,1)S(1)} %get-tuple-element.1678) | copy-start | bytes 2359300
  691.5 123.5 %collective-permute-start.3 = (bf16[768,512]{1,0:T(8,128)(2,1)S(1)}, bf16[768,512]{1,0:T(8,128)(2,1)}, u32[]{:S(2)}, u32[]{:S(2)}) collective-permute-start(bf16[768,512]{1,0:T(8,128)(2,1)S(1)} %get-tuple-element.1678), channel_id=1, source_target_pairs={{64,0},{65,1},{66,2},{67,3},{68,4},{69,5},{70,6},{71,7},{72,8},{73... | collective-permute-start | bytes 2359304 | tf_op jit(solution)/shard_map/ppermute | solution.py:25
  994.3 91.0 %copy-start.38 = (bf16[768,8,64]{0,2,1:T(8,128)(2,1)S(1)}, bf16[768,8,64]{0,2,1:T(8,128)(2,1)}, u32[]{:S(2)}) copy-start(bf16[768,8,64]{0,2,1:T(8,128)(2,1)} %copy-done.37) | copy-start | bytes 2359300
  994.3 91.0 %copy-start.40 = (bf16[768,8,64]{0,2,1:T(8,128)(2,1)S(1)}, bf16[768,8,64]{0,2,1:T(8,128)(2,1)}, u32[]{:S(2)}) copy-start(bf16[768,8,64]{0,2,1:T(8,128)(2,1)} %copy-done.39) | copy-start | bytes 2359300
  994.3 91.0 %copy-start.55 = (bf16[768,512]{1,0:T(8,128)(2,1)S(1)}, bf16[768,512]{1,0:T(8,128)(2,1)}, u32[]{:S(2)}) copy-start(bf16[768,512]{1,0:T(8,128)(2,1)} %get-tuple-element.783) | copy-start | bytes 2359300
  994.3 91.0 %copy-start.58 = (bf16[768,512]{1,0:T(8,128)(2,1)S(1)}, bf16[768,512]{1,0:T(8,128)(2,1)}, u32[]{:S(2)}) copy-start(bf16[768,512]{1,0:T(8,128)(2,1)} %get-tuple-element.797) | copy-start | bytes 2359300
  994.3 129.9 %all-reduce.34.cloned.1.call-start = ((), (), s32[]{:S(2)}) async-start(), calls=%async_computation.27 | async-start | bytes 218112 | tf_op jit(solution)/shard_map/psum | solution.py:467
  1084.4 117.9 %reduce-scatter.13.cloned.1.call-start = ((), (), s32[]{:S(2)}) async-start(), calls=%async_computation.15 | async-start | bytes 1671168 | tf_op jit(solution)/shard_map/reduce_scatter | solution.py:425
  1085.2 193.4 %reduce-scatter.15.cloned.1.call-start = ((), (), s32[]{:S(2)}) async-start(), calls=%async_computation.16 | async-start | bytes 1671168 | tf_op jit(solution)/shard_map/reduce_scatter | solution.py:425
  1089.1 266.4 %reduce-scatter.25.cloned.1.call-start = ((), (), s32[]{:S(2)}) async-start(), calls=%async_computation.21 | async-start | bytes 2228224 | tf_op jit(solution)/shard_map/reduce_scatter | solution.py:440
  1089.7 343.1 %reduce-scatter.31.cloned.1.call-start = ((), (), s32[]{:S(2)}) async-start(), calls=%async_computation.24 | async-start | bytes 2228224 | tf_op jit(solution)/shard_map/reduce_scatter | solution.py:446
  1090.4 418.4 %reduce-scatter.17.cloned.1.call-start = ((), (), s32[]{:S(2)}) async-start(), calls=%async_computation.17 | async-start | bytes 1671168 | tf_op jit(solution)/shard_map/reduce_scatter | solution.py:425
  1091.0 495.0 %reduce-scatter.27.cloned.1.call-start = ((), (), s32[]{:S(2)}) async-start(), calls=%async_computation.22 | async-start | bytes 2228224 | tf_op jit(solution)/shard_map/reduce_scatter | solution.py:440
  1096.4 566.8 %reduce-scatter.33.cloned.1.call-start = ((), (), s32[]{:S(2)}) async-start(), calls=%async_computation.25 | async-start | bytes 2228224 | tf_op jit(solution)/shard_map/reduce_scatter | solution.py:446
  1114.2 625.8 %reduce-scatter.29.cloned.1.call-start = ((), (), s32[]{:S(2)}) async-start(), calls=%async_computation.23 | async-start | bytes 2228224 | tf_op jit(solution)/shard_map/reduce_scatter | solution.py:440
  1114.8 702.4 %reduce-scatter.35.cloned.1.call-start = ((), (), s32[]{:S(2)}) async-start(), calls=%async_computation.26 | async-start | bytes 2228224 | tf_op jit(solution)/shard_map/reduce_scatter | solution.py:446
  1115.4 750.8 %all-reduce.36.cloned.1.call-start = ((), (), s32[]{:S(2)}) async-start(), calls=%async_computation.28 | async-start | bytes 2162688 | tf_op jit(solution)/shard_map/psum | solution.py:469
  (111 other events, 472.1 us)
Sparse Core Ops, SparseCore 0:
  10.2 46.6 all-gather.3
  59.0 44.6 all-gather.5
  105.8 44.5 all-gather.7
  362.9 248.0 reduce-scatter.18
  687.4 191.5 reduce-scatter.20
  994.4 71.6 reduce-scatter.22
  1084.5 39.6 all-reduce.33
  1127.5 74.7 reduce-scatter.12
  1205.5 73.0 reduce-scatter.14
  1281.7 73.7 reduce-scatter.24
  1359.1 73.6 reduce-scatter.30
  1435.9 72.8 reduce-scatter.16
  1512.1 73.8 reduce-scatter.26
  1589.4 73.7 reduce-scatter.32
  1666.3 73.6 reduce-scatter.28
  1743.5 73.6 reduce-scatter.34
  1820.0 46.0 all-reduce.35
where the time goes:
time: 1890 us; the launch traced here: 1880 us
  waiting for transfers between devices  1050 us (56%)
  matrix products  335 us (18%)
  blocking collectives  159 us (8%)
  local copies, waits for them, and re-layouts  151 us (8%)
  other arithmetic  88.8 us (5%)
  loops' own time  65.6 us (3%)
  between operations  19 us (1%)
    ppermute x4, waiting for transfers between devices, passed_along(): lax.ppermute(value, axis, [(source, source + steps) for source in range(i...  272 us
    reduce_scatter x3, waiting for transfers between devices, body(): lax.psum_scatter(grad_narrow_matrix.astype(jnp.bfloat16), 'shard', scatte...  232 us
    reduce_scatter x3, waiting for transfers between devices, body(): lax.psum_scatter(grad_widen_matrix.astype(jnp.bfloat16), 'shard', scatter...  231 us
    reduce_scatter x3, waiting for transfers between devices, body(): lax.psum_scatter(grad_attend_matrix.astype(jnp.bfloat16), 'shard', scatte...  227 us
    unnamed x1, blocking collectives  73 us
    dot_general x32, matrix products, one_head(): jnp.dot(head_query, head_key.T, preferred_element_type=jnp.float32)  52.2 us
    squeeze x1, blocking collectives, fetch_forward(): return tuple((member[0] for member in members))  43 us
    psum x1, waiting for transfers between devices, body(): lax.psum(share_attend_matrix.astype(jnp.bfloat16), 'replica')  42.8 us
  transfers between devices with their start and end apart: 21, of which 15 were waited for; matrix products, arithmetic and copies ran while one was open for 21% of the time, Pallas kernels for 0%

commit v1 on v0

v1 whole, which is shorter than its diff:
```python
import math

import jax
import jax.numpy as jnp
from jax import lax
from jax.experimental import pallas as pl
from jax.experimental.pallas import tpu as pltpu
from jax.sharding import PartitionSpec as P

T = 768
D = 512
FF = 2048
HEADS = 8
HEAD = 64
ROT = 16
BLOCK = 128
SEQS = 4
TILE = 256
EPS = 1e-5
MASKED = -1e9
LOG2E = 1.0 / math.log(2.0)
LN2 = math.log(2.0)
MESH = pl.DeviceIdType.MESH
BF = jnp.bfloat16
F32 = jnp.float32

QKV, DENSE, FIN, FOUT, VEC = range(5)
HALF_ROWS = (16, 16, 16, 64, 8)
WIDTH = (1536, 512, 2048, 512, 128)
KIND = (BF, BF, BF, BF, F32)


def dg(a, b, ca, cb):
    return lax.dot_general(a, b, (((ca,), (cb,)), ((), ())), preferred_element_type=F32)


class Place:
    def __init__(self):
        self.s = lax.axis_index("section")
        self.y = lax.axis_index("replica")
        shard = lax.axis_index("shard")
        x, z = shard // 4, shard % 4
        self.shard = shard
        self.p = x + self.s * (z - x)
        self.q = z + self.s * (x - z)

    def at(self, p, q):
        return (1 - self.s) * (4 * p + q) + self.s * (4 * q + p)

    def sibling(self):
        return (1 - self.s, self.y, self.shard)

    def along_p(self, d):
        return (self.s, self.y, self.at((self.p + d) % 4, self.q))

    def along_q(self, d):
        return (self.s, self.y, self.at(self.p, (self.q + d) % 4))

    def along_y(self, d):
        return (self.s, (self.y + d) % 4, self.shard)


def remote(src, dst, send, recv, device):
    return pltpu.make_async_remote_copy(
        src_ref=src, dst_ref=dst, send_sem=send, recv_sem=recv, device_id=device, device_id_type=MESH
    )


class Gather:
    def __init__(self, me, layer, part, shard_ref, whole, send, recv, local):
        self.me, self.layer, self.part = me, layer, part
        self.shard_ref, self.w = shard_ref, whole
        self.send = lambda k: send.at[layer, part, k]
        self.recv = lambda k: recv.at[layer, part, k]
        self.local = local.at[part]
        self.rows = HALF_ROWS[part]

    def half(self, h):
        if self.part == VEC:
            return self.shard_ref.at[h]
        return self.shard_ref.at[0, pl.ds(pl.multiple_of(h * self.rows, self.rows), self.rows), :]

    def own_copy(self):
        me = self.me
        return pltpu.make_async_copy(self.half(me.s), self.w.at[me.s, me.p, me.q], self.local)

    def hand_over(self):
        me = self.me
        return remote(
            self.half(1 - me.s), self.w.at[1 - me.s, me.q, me.p], self.send(0), self.recv(0), me.sibling()
        )

    def first(self, d):
        me = self.me
        own = self.w.at[me.s, me.p, me.q]
        return remote(own, own, self.send(d), self.recv(d), me.along_q(d))

    def first_landing(self, d):
        me = self.me
        there = self.w.at[me.s, me.p, (me.q + 4 - d) % 4]
        return remote(there, there, self.send(d), self.recv(d), me.along_q(d))

    def second(self, d):
        me = self.me
        row = self.w.at[me.s, me.p]
        return remote(row, row, self.send(3 + d), self.recv(3 + d), me.along_p(d))

    def second_landing(self, d):
        me = self.me
        row = self.w.at[me.s, (me.p + 4 - d) % 4]
        return remote(row, row, self.send(3 + d), self.recv(3 + d), me.along_p(d))

    def across(self, d):
        me = self.me
        row = self.w.at[me.s, (me.p + 4 - d) % 4]
        return remote(row, row, self.send(7 + d), self.recv(7 + d), me.sibling())

    def across_landing(self, d):
        me = self.me
        row = self.w.at[1 - me.s, (me.q + 4 - d) % 4]
        return remote(row, row, self.send(7 + d), self.recv(7 + d), me.sibling())

    def step0(self):
        @pl.when(self.me.s == self.layer)
        def _():
            self.own_copy().start()
            self.hand_over().start()

    def step1(self):
        @pl.when(self.me.s == self.layer)
        def _():
            self.own_copy().wait()

        @pl.when(self.me.s != self.layer)
        def _():
            me = self.me
            own = self.w.at[me.s, me.p, me.q]
            remote(own, own, self.send(0), self.recv(0), me.sibling()).wait_recv()

        for d in (1, 3, 2):
            self.first(d).start()

    def step2(self):
        for d in (1, 3, 2):
            self.first_landing(d).wait_recv()
        for d in (1, 3, 2):
            self.second(d).start()
        self.across(0).start()

    def step3(self):
        for d in (1, 3, 2):
            self.second_landing(d).wait_recv()
            self.across(d).start()

    def step4(self):
        for d in range(4):
            self.across_landing(d).wait_recv()

    def finish(self):
        @pl.when(self.me.s == self.layer)
        def _():
            self.hand_over().wait_send()

        for d in (1, 2, 3):
            self.first(d).wait_send()
            self.second(d).wait_send()
        for d in range(4):
            self.across(d).wait_send()


class Reduce:
    def __init__(self, me, layer, part, terms, buffers, send, recv):
        self.me, self.layer, self.part = me, layer, part
        self.g = terms
        self.r, self.one, self.two, self.ys, self.f, self.out = buffers
        self.send = lambda k: send.at[layer, part, k]
        self.recv = lambda k: recv.at[layer, part, k]
        self.kind = KIND[part]

    def swap(self):
        me = self.me
        return remote(self.g.at[1 - me.s], self.r, self.send(0), self.recv(0), me.sibling())

    def first(self, d):
        me = self.me
        return remote(
            self.r.at[(me.p + d) % 4], self.one.at[d - 1], self.send(d), self.recv(d), me.along_p(d)
        )

    def second(self, d):
        me = self.me
        return remote(
            self.r.at[me.p, (me.q + d) % 4],
            self.two.at[d - 1],
            self.send(3 + d),
            self.recv(3 + d),
            me.along_q(d),
        )

    def third(self, d):
        me = self.me
        return remote(
            self.ys.at[me.y], self.ys.at[me.y], self.send(6 + d), self.recv(6 + d), me.along_y(d)
        )

    def third_landing(self, d):
        me = self.me
        there = self.ys.at[(me.y + 4 - d) % 4]
        return remote(there, there, self.send(6 + d), self.recv(6 + d), me.along_y(d))

    def back(self):
        me = self.me
        return remote(self.f, self.out.at[me.s], self.send(10), self.recv(10), me.sibling())

    def step0(self):
        self.swap().start()

    def step1(self):
        me = self.me
        self.swap().wait_recv()

        def one(k, c):
            a, b = k // 4, k % 4
            self.r[a, b] = (self.r[a, b].astype(F32) + self.g[me.s, a, b].astype(F32)).astype(self.kind)
            return c

        lax.fori_loop(0, 16, one, 0)
        for d in (1, 3, 2):
            self.first(d).start()
        self.swap().wait_send()

    def step2(self):
        me = self.me
        for d in (1, 2, 3):
            self.first(d).wait_recv()

        def one(b, c):
            total = self.r[me.p, b].astype(F32) + self.one[0, b].astype(F32)
            total = total + (self.one[1, b].astype(F32) + self.one[2, b].astype(F32))
            self.r[me.p, b] = total.astype(self.kind)
            return c

        lax.fori_loop(0, 4, one, 0)
        for d in (1, 3, 2):
            self.second(d).start()

    def step3(self):
        me = self.me
        for d in (1, 2, 3):
            self.second(d).wait_recv()
        total = self.r[me.p, me.q].astype(F32) + self.two[0].astype(F32)
        total = total + (self.two[1].astype(F32) + self.two[2].astype(F32))
        self.ys[me.y] = total.astype(self.kind)
        for d in (1, 3, 2):
            self.third(d).start()

    def step4(self):
        me = self.me
        for d in (1, 2, 3):
            self.third_landing(d).wait_recv()
        total = (self.ys[0].astype(F32) + self.ys[1].astype(F32)) + (
            self.ys[2].astype(F32) + self.ys[3].astype(F32)
        )

        @pl.when(me.s == self.layer)
        def _():
            self.out[me.s] = total

        @pl.when(me.s != self.layer)
        def _():
            self.f[...] = total
            self.back().start()

    def step5(self):
        me = self.me

        @pl.when(me.s == self.layer)
        def _():
            there = self.out.at[1 - me.s]
            remote(there, there, self.send(10), self.recv(10), me.sibling()).wait_recv()

    def finish(self):
        for d in (1, 2, 3):
            self.first(d).wait_send()
            self.second(d).wait_send()
            self.third(d).wait_send()

        @pl.when(self.me.s != self.layer)
        def _():
            self.back().wait_send()


def natural_rows(ref, columns):
    pieces = []
    for x in range(4):
        for z in range(4):
            pieces.append(ref[0, x, z, :, columns])
            pieces.append(ref[1, z, x, :, columns])
    return jnp.concatenate(pieces, axis=0)


def group_rows(ref, x):
    pieces = []
    for z in range(4):
        pieces.append(ref[0, x, z])
        pieces.append(ref[1, z, x])
    return jnp.concatenate(pieces, axis=0)


def put_natural(ref, columns, value):
    for x in range(4):
        for z in range(4):
            row = 32 * (4 * x + z)
            ref[0, x, z, :, columns] = value[row : row + 16]
            ref[1, z, x, :, columns] = value[row + 16 : row + 32]


def put_group(ref, x, value, rows):
    for z in range(4):
        row = 2 * rows * z
        ref[0, x, z] = value[row : row + rows]
        ref[1, z, x] = value[row + rows : row + 2 * rows]


def to_column(row):
    here = lax.broadcasted_iota(jnp.int32, (128, 128), 0) == lax.broadcasted_iota(
        jnp.int32, (128, 128), 1
    )
    return jnp.sum(jnp.where(here, row, 0.0), axis=1, keepdims=True)


def turn(rows, cosine, sine):
    pieces = []
    for e in (0, 64):
        low, high = rows[e : e + 8], rows[e + 8 : e + 16]
        pieces += [low * cosine - high * sine, high * cosine + low * sine, rows[e + 16 : e + 64]]
    return jnp.concatenate(pieces, axis=0)


def columns(start, size):
    return pl.ds(pl.multiple_of(start, size), size)


def loop(count, step):
    def one(k, c):
        step(k)
        return c

    lax.fori_loop(0, count, one, 0)


def kernel(
    lengths,
    x_ref,
    cot_ref,
    wq_ref,
    wd_ref,
    wi_ref,
    wo_ref,
    vec_ref,
    act_out,
    ig_out,
    gq_out,
    gd_out,
    gi_out,
    go_out,
    gv_out,
    st_qkv,
    st_p0,
    st_p1,
    st_p2,
    st_bt,
    st_rinv,
    st_act,
    st_slo,
    *scratch,
):
    scratch = list(scratch)

    def take(count):
        taken, scratch[:count] = scratch[:count], []
        return taken

    w = [take(5), take(5)]
    g = take(5)
    r = [take(5), take(5)]
    one = [take(5), take(5)]
    two = [take(5), take(5)]
    ys = [take(5), take(5)]
    f = take(5)
    hid, grad, n1t, n2, acc, carried = take(6)
    qkvt, p0, p1, p2, bt, rinv, act, slo = take(8)
    d0, d1, d2, dn1 = take(4)
    vd, vq, vf, dvec, fvec, live, bias, cos_ref, sin_ref = take(9)
    ag_send, ag_recv, rs_send, rs_recv, ag_local, sems, ex_send, ex_recv = take(8)
    probs = (p0, p1, p2)
    dscores = (d0, d1, d2)
    outs = (gq_out, gd_out, gi_out, go_out, gv_out)
    shards = (wq_ref, wd_ref, wi_ref, wo_ref, vec_ref)

    me = Place()
    s = me.s
    barrier = pltpu.get_barrier_semaphore()
    partners = [me.sibling()]
    for d in (1, 2, 3):
        partners += [me.along_q(d), me.along_p(d), me.along_y(d)]
    for device in partners:
        pl.semaphore_signal(barrier, inc=1, device_id=device, device_id_type=MESH)
    pl.semaphore_wait(barrier, len(partners))

    gather = [
        [Gather(me, l, c, shards[c], w[l][c], ag_send, ag_recv, ag_local) for c in range(5)]
        for l in (0, 1)
    ]
    reduce = [
        [
            Reduce(
                me, l, c, g[c], (r[l][c], one[l][c], two[l][c], ys[l][c], f[c], outs[c]), rs_send, rs_recv
            )
            for c in range(5)
        ]
        for l in (0, 1)
    ]
    order = (VEC, QKV, DENSE, FIN, FOUT)

    x_in = pltpu.make_async_copy(x_ref.at[s], hid.at[0], sems.at[0])
    cot_in = pltpu.make_async_copy(cot_ref.at[s], grad.at[2], sems.at[1])
    x_in.start()
    for l in (0, 1):
        for c in order:
            gather[l][c].step0()
    for c in order:
        gather[0][c].step1()
    cot_in.start()

    starts, ends, at = [], [], jnp.int32(0)
    for k in range(SEQS):
        size = lengths[s, 0, k]
        starts.append(at)
        ends.append(at + size)
        at = at + (size + BLOCK - 1) // BLOCK * BLOCK

    def inside(places):
        return [(places >= a) & (places < b) for a, b in zip(starts, ends)]

    def live_tile(k):
        places = lax.broadcasted_iota(jnp.int32, (TILE, 1), 0) + k * TILE
        total = jnp.zeros((TILE, 1), F32)
        for found in inside(places):
            total = total + jnp.where(found, 1.0, 0.0)
        live[columns(k * TILE, TILE), :] = total

    loop(3, live_tile)
    places = lax.broadcasted_iota(jnp.int32, (8, T), 1)
    begin = jnp.zeros((8, T), jnp.int32)
    offset = jnp.zeros((8, T), jnp.int32)
    for found, a in zip(inside(places), starts):
        begin = begin + jnp.where(found, a, 0)
        offset = offset + jnp.where(found, places - a, 0)
    rates = jnp.exp(
        lax.broadcasted_iota(jnp.int32, (8, T), 0).astype(F32) * (-2.0 * math.log(10000.0) / ROT)
    )
    angles = offset.astype(F32) * rates
    cos_ref[...] = jnp.cos(angles)
    sin_ref[...] = jnp.sin(angles)
    for j in range(3):
        for i in range(j + 1):
            keys = lax.broadcasted_iota(jnp.int32, (TILE, TILE), 0) + i * TILE
            queries = lax.broadcasted_iota(jnp.int32, (TILE, TILE), 1) + j * TILE
            fits = (keys >= begin[0:1, j * TILE : (j + 1) * TILE]) & (keys <= queries)
            bias[j * (j + 1) // 2 + i] = jnp.where(fits, 0.0, MASKED)

    def unpack(l):
        ref = w[l][VEC]
        for x in range(4):
            vd[:, 128 * x : 128 * x + 128] = (ref[0, x, 0] + ref[0, x, 1]) + (ref[0, x, 2] + ref[0, x, 3])
            group = (ref[1, 0, x] + ref[1, 1, x]) + (ref[1, 2, x] + ref[1, 3, x])
            for k in range(3):
                vq[3 * x + k : 3 * x + k + 1, :] = group[k : k + 1]
            for z in range(4):
                vf[x : x + 1, 128 * z : 128 * z + 128] = ref[1, z, x][3:4]

    def normed(l, rows):
        v = hid[l, rows, :].astype(F32)
        centred = v - jnp.mean(v, axis=1, keepdims=True)
        scale = lax.rsqrt(jnp.mean(centred * centred, axis=1, keepdims=True) + EPS)
        return centred * scale, scale

    def norms(l):
        def tile(k):
            rows = columns(k * TILE, TILE)
            u, _ = normed(l, rows)
            n1t[:, rows] = (u * vd[0:1, :] + vd[1:2, :]).astype(BF).T
            n2[rows, :] = (u * vd[2:3, :] + vd[3:4, :]).astype(BF)

        loop(3, tile)

    def attend(l, hp):
        pair = []
        for which in range(3):
            rows = columns(which * D + hp * 128, 128)
            weight = natural_rows(w[l][QKV], rows)
            value = dg(weight, n1t[...], 0, 0) + to_column(vq[pl.ds(which * 4 + hp, 1), :])
            if which < 2:
                value = turn(value, cos_ref[...], sin_ref[...])
            if which == 0:
                value = value * (LOG2E / 8.0)
            pair.append(value.astype(BF))
            qkvt[rows, :] = pair[which]
        keys = pair[1].T
        blank = jnp.zeros((HEAD, TILE), BF)
        for e in (0, 1):
            h = 2 * hp + e
            query = pair[0][e * HEAD : (e + 1) * HEAD]
            value = pair[2][e * HEAD : (e + 1) * HEAD]
            for j in range(3):
                at_j = slice(j * TILE, (j + 1) * TILE)
                mine = query[:, at_j]
                mine = jnp.concatenate([mine, blank] if e == 0 else [blank, mine], axis=0)
                scores = [
                    dg(keys[i * TILE : (i + 1) * TILE], mine, 1, 0) + bias[j * (j + 1) // 2 + i]
                    for i in range(j + 1)
                ]
                peak = jnp.max(scores[0], axis=0, keepdims=True)
                for i in range(1, j + 1):
                    peak = jnp.maximum(peak, jnp.max(scores[i], axis=0, keepdims=True))
                total = jnp.zeros((1, TILE), F32)
                blended = jnp.zeros((HEAD, TILE), F32)
                for i in range(j + 1):
                    raised = jnp.exp2(scores[i] - peak)
                    total = total + jnp.sum(raised, axis=0, keepdims=True)
                    raised = raised.astype(BF)
                    probs[i][h, :, (j - i) * TILE : (j - i + 1) * TILE] = raised
                    blended = blended + dg(value[:, i * TILE : (i + 1) * TILE], raised, 1, 0)
                inverse = 1.0 / total
                rinv[pl.ds(h, 1), at_j] = inverse
                bt[columns(hp * 128 + e * HEAD, HEAD), at_j] = (blended * inverse).astype(BF)

    def widen(l, c):
        cols = columns(c * 512, 512)
        weight = natural_rows(w[l][FIN], cols)
        shift = vf[pl.ds(c, 1), :]

        def tile(k):
            rows = columns(k * TILE, TILE)
            v = dg(n2[rows, :], weight, 1, 0) + shift
            below = 0.5 + 0.5 * lax.erf(v * (1.0 / math.sqrt(2.0)))
            act[rows, cols] = (v * below).astype(BF)
            slope = below + v * (jnp.exp(-0.5 * v * v) * (1.0 / math.sqrt(2.0 * math.pi)))
            slo[rows, cols] = slope.astype(BF)

        for k in range(3):
            tile(k)

    def join(l):
        def part(t):
            cols = columns(t * TILE, TILE)
            weight = jnp.concatenate(
                [
                    piece
                    for x in range(4)
                    for z in range(4)
                    for piece in (w[l][FOUT][0, x, z, :, cols], w[l][FOUT][1, z, x, :, cols])
                ],
                axis=0,
            )
            total = dg(act[...], weight, 1, 0)
            total = total + dg(bt[...], natural_rows(w[l][DENSE], cols), 0, 0)
            total = total + hid[l, :, cols].astype(F32) + vd[4:5, cols]
            hid[l + 1, :, cols] = (total * live[...]).astype(BF)

        loop(2, part)

    def local(src, dst, k):
        return pltpu.make_async_copy(src, dst, sems.at[k])

    attention_kept = [
        (qkvt, st_qkv, 2),
        (p0, st_p0, 3),
        (p1, st_p1, 4),
        (p2, st_p2, 5),
        (bt, st_bt, 6),
        (rinv, st_rinv, 7),
    ]
    wide_kept = [(act, st_act, 8), (slo, st_slo, 9)]

    for c in order:
        gather[0][c].step2()
    for c in order:
        gather[1][c].step1()
    x_in.wait()
    gather[0][VEC].step3()
    gather[0][VEC].step4()
    unpack(0)
    norms(0)
    gather[0][QKV].step3()
    gather[0][QKV].step4()
    loop(2, lambda hp: attend(0, hp))
    for c in (DENSE, FIN, FOUT):
        gather[0][c].step3()
    for c in order:
        gather[1][c].step2()
    loop(2, lambda hp: attend(0, hp + 2))
    for a, b, k in attention_kept:
        local(a, b, k).start()
    for c in (DENSE, FIN, FOUT):
        gather[0][c].step4()
    loop(4, lambda c: widen(0, c))
    for c in order:
        gather[1][c].step3()
    join(0)
    for a, b, k in wide_kept:
        local(a, b, k).start()
    for c in (VEC, QKV, DENSE):
        gather[1][c].step4()

    unpack(1)
    norms(1)
    for a, b, k in attention_kept:
        local(a, b, k).wait()
    loop(4, lambda hp: attend(1, hp))
    for c in (FIN, FOUT):
        gather[1][c].step4()
    for a, b, k in wide_kept:
        local(a, b, k).wait()
    loop(4, lambda c: widen(1, c))
    join(1)
    for l in (0, 1):
        for c in order:
            gather[l][c].finish()
    act_mine = local(hid.at[1 + s], act_out.at[s], 10)
    act_theirs = remote(hid.at[2 - s], act_out.at[s], ex_send.at[0], ex_recv.at[0], me.sibling())
    act_mine.start()
    act_theirs.start()
    cot_in.wait()

    def start_back(l):
        def tile(k):
            rows = columns(k * TILE, TILE)
            v = grad[l + 1, rows, :].astype(F32) * live[rows, :]
            carried[rows, :] = v.astype(BF)
            here = jnp.sum(v, axis=0, keepdims=True)
            dvec[4:5, :] = here + jnp.where(k == 0, 0.0, dvec[4:5, :])

        dvec[...] = jnp.zeros((8, D), F32)
        loop(3, tile)

    def back_out(l, c):
        cols = columns(c * 512, 512)
        put_group(g[FOUT], c, dg(act[:, cols], carried[...], 0, 0).astype(BF), 64)
        weight = group_rows(w[l][FOUT], c)
        total = jnp.zeros((1, 512), F32)
        for k in range(3):
            rows = slice(k * TILE, (k + 1) * TILE)
            v = dg(carried[rows, :], weight, 1, 1) * slo[rows, cols].astype(F32)
            v = v.astype(BF)
            slo[rows, cols] = v
            total = total + jnp.sum(v.astype(F32), axis=0, keepdims=True)
        fvec[pl.ds(c, 1), :] = total

    def back_in(l, c):
        cols = columns(c * 512, 512)
        put_natural(g[FIN], cols, dg(n2[...], slo[:, cols], 0, 0).astype(BF))

    def back_norm_two(l, t):
        cols = columns(t * TILE, TILE)
        pieces = []
        for x in range(2):
            for z in range(4):
                pieces.append(w[l][FIN][0, 2 * t + x, z])
                pieces.append(w[l][FIN][1, z, 2 * t + x])
        acc[:, cols] = dg(slo[...], jnp.concatenate(pieces, axis=0), 1, 1)

    def back_dense(l):
        put_natural(g[DENSE], slice(0, 512), dg(bt[...], carried[...], 1, 0).astype(BF))

    def back_attend(l, hp):
        weight = group_rows(w[l][DENSE], hp)
        below = dg(weight, carried[...], 1, 1)
        queries = qkvt[columns(hp * 128, 128), :]
        keys = qkvt[columns(D + hp * 128, 128), :]
        values = qkvt[columns(2 * D + hp * 128, 128), :].T
        blended = bt[columns(hp * 128, 128), :].astype(F32)
        blank = jnp.zeros((HEAD, TILE), BF)
        done = []
        for e in (0, 1):
            h = 2 * hp + e
            query = queries[e * HEAD : (e + 1) * HEAD]
            key = keys[e * HEAD : (e + 1) * HEAD]
            down = below[e * HEAD : (e + 1) * HEAD] * rinv[pl.ds(h, 1), :]
            centre = jnp.sum(down * blended[e * HEAD : (e + 1) * HEAD], axis=0, keepdims=True)
            down = down.astype(BF)
            grad_query = []
            for j in range(3):
                at_j = slice(j * TILE, (j + 1) * TILE)
                mine = down[:, at_j]
                mine = jnp.concatenate([mine, blank] if e == 0 else [blank, mine], axis=0)
                total = jnp.zeros((HEAD, TILE), F32)
                for i in range(j + 1):
                    cols = slice((j - i) * TILE, (j - i + 1) * TILE)
                    slope = dg(values[i * TILE : (i + 1) * TILE], mine, 1, 0) - centre[:, at_j]
                    slope = (slope * probs[i][h, :, cols].astype(F32)).astype(BF)
                    dscores[i][:, cols] = slope
                    total = total + dg(key[:, i * TILE : (i + 1) * TILE], slope, 1, 0)
                grad_query.append(total * 0.125)
            grad_key, grad_value = [], []
            for i in range(3):
                grad_key.append(dg(query[:, i * TILE :], dscores[i][...], 1, 1) * LN2)
                grad_value.append(dg(down[:, i * TILE :], probs[i][h], 1, 1))
            done.append(
                [jnp.concatenate(pieces, axis=1) for pieces in (grad_query, grad_key, grad_value)]
            )
        for which in range(3):
            value = jnp.concatenate([done[0][which], done[1][which]], axis=0)
            if which < 2:
                value = turn(value, cos_ref[...], -sin_ref[...])
            qkvt[columns(which * D + hp * 128, 128), :] = value.astype(BF)

    def back_qkv(l, t):
        cols = columns(t * 512, 512)
        put_natural(g[QKV], cols, dg(n1t[...], qkvt[cols, :], 1, 1).astype(BF))

    def back_norm_one(l, t):
        weight = group_rows(w[l][QKV], t)
        dn1[:, columns(t * 128, 128)] = dg(weight, qkvt[...], 1, 0).astype(BF).T

    def end_back(l):
        def tile(k):
            rows = columns(k * TILE, TILE)
            u, scale = normed(l, rows)
            first = dn1[rows, :].astype(F32)
            second = acc[rows, :]
            dvec[0:1, :] += jnp.sum(first * u, axis=0, keepdims=True)
            dvec[1:2, :] += jnp.sum(first, axis=0, keepdims=True)
            dvec[2:3, :] += jnp.sum(second * u, axis=0, keepdims=True)
            dvec[3:4, :] += jnp.sum(second, axis=0, keepdims=True)
            total = first * vd[0:1, :] + second * vd[2:3, :]
            centre = jnp.mean(total, axis=1, keepdims=True)
            along = jnp.mean(total * u, axis=1, keepdims=True)
            total = carried[rows, :].astype(F32) + scale * (total - centre - u * along)
            grad[l, rows, :] = total.astype(BF)

        loop(3, tile)

    def put_vectors(l):
        sums = dg(jnp.ones((8, T), BF), qkvt[...], 1, 1)
        g[VEC][...] = jnp.zeros((2, 4, 4, 8, 128), F32)
        for x in range(4):
            for z in range(4):
                g[VEC][0, x, z] = dvec[:, 128 * x : 128 * x + 128]
                for k in range(3):
                    row = 128 * (3 * x + k)
                    g[VEC][1, z, x, k : k + 1, :] = sums[0:1, row : row + 128]
                g[VEC][1, z, x, 3:4, :] = fvec[x : x + 1, 128 * z : 128 * z + 128]

    start_back(1)
    loop(4, lambda c: back_out(1, c))
    reduce[1][FOUT].step0()
    loop(4, lambda c: back_in(1, c))
    reduce[1][FIN].step0()
    reduce[1][FOUT].step1()
    loop(2, lambda t: back_norm_two(1, t))
    local(st_act, act, 8).start()
    local(st_slo, slo, 9).start()
    back_dense(1)
    reduce[1][DENSE].step0()
    reduce[1][FIN].step1()
    loop(2, lambda hp: back_attend(1, hp))
    reduce[1][FOUT].step2()
    reduce[1][DENSE].step1()
    loop(2, lambda hp: back_attend(1, hp + 2))
    reduce[1][FIN].step2()
    reduce[1][FOUT].step3()
    loop(3, lambda t: back_qkv(1, t))
    reduce[1][QKV].step0()
    loop(4, lambda t: back_norm_one(1, t))
    end_back(1)
    put_vectors(1)
    reduce[1][VEC].step0()
    for k, (a, b) in zip((2, 3, 4, 5, 6, 7), ((st_qkv, qkvt), (st_p0, p0), (st_p1, p1), (st_p2, p2), (st_bt, bt), (st_rinv, rinv))):
        local(a, b, k).start()
    reduce[1][QKV].step1()
    reduce[1][VEC].step1()
    reduce[1][DENSE].step2()

    unpack(0)
    norms(0)
    start_back(0)
    local(st_act, act, 8).wait()
    local(st_slo, slo, 9).wait()
    loop(4, lambda c: back_out(0, c))
    reduce[0][FOUT].step0()
    reduce[1][FIN].step3()
    reduce[1][FOUT].step4()
    loop(4, lambda c: back_in(0, c))
    reduce[0][FIN].step0()
    reduce[0][FOUT].step1()
    reduce[1][DENSE].step3()
    reduce[1][QKV].step2()
    reduce[1][VEC].step2()
    reduce[1][FIN].step4()
    loop(2, lambda t: back_norm_two(0, t))
    for k, (a, b) in zip((2, 3, 4, 5, 6, 7), ((st_qkv, qkvt), (st_p0, p0), (st_p1, p1), (st_p2, p2), (st_bt, bt), (st_rinv, rinv))):
        local(a, b, k).wait()
    back_dense(0)
    reduce[0][DENSE].step0()
    reduce[0][FIN].step1()
    loop(2, lambda hp: back_attend(0, hp))
    reduce[0][FOUT].step2()
    reduce[0][DENSE].step1()
    reduce[1][QKV].step3()
    reduce[1][VEC].step3()
    reduce[1][DENSE].step4()
    loop(2, lambda hp: back_attend(0, hp + 2))
    reduce[0][FIN].step2()
    reduce[0][FOUT].step3()
    loop(3, lambda t: back_qkv(0, t))
    reduce[0][QKV].step0()
    reduce[0][DENSE].step2()
    reduce[1][QKV].step4()
    reduce[1][VEC].step4()
    loop(4, lambda t: back_norm_one(0, t))
    reduce[0][QKV].step1()
    end_back(0)
    put_vectors(0)
    reduce[0][VEC].step0()
    grad_mine = local(grad.at[s], ig_out.at[s], 11)
    grad_theirs = remote(grad.at[1 - s], ig_out.at[s], ex_send.at[1], ex_recv.at[1], me.sibling())
    grad_mine.start()
    grad_theirs.start()
    reduce[0][FIN].step3()
    reduce[0][FOUT].step4()
    reduce[0][VEC].step1()
    reduce[0][DENSE].step3()
    reduce[0][FIN].step4()
    reduce[0][QKV].step2()
    reduce[0][VEC].step2()
    reduce[0][DENSE].step4()
    reduce[0][QKV].step3()
    reduce[0][VEC].step3()
    reduce[0][QKV].step4()
    reduce[0][VEC].step4()
    for l in (1, 0):
        for c in order:
            reduce[l][c].step5()
            reduce[l][c].finish()
    act_mine.wait()
    act_theirs.wait_send()
    remote(hid.at[2 - s], act_out.at[1 - s], ex_send.at[0], ex_recv.at[0], me.sibling()).wait_recv()
    grad_mine.wait()
    grad_theirs.wait_send()
    remote(grad.at[1 - s], ig_out.at[1 - s], ex_send.at[1], ex_recv.at[1], me.sibling()).wait_recv()


def scratch_shapes():
    def parts(lead):
        return [
            pltpu.VMEM((*lead, HALF_ROWS[c], WIDTH[c]), KIND[c]) for c in range(5)
        ]

    shapes = []
    for _ in (0, 1):
        shapes += parts((2, 4, 4))
    shapes += parts((2, 4, 4))
    for _ in (0, 1):
        shapes += parts((4, 4))
    for _ in (0, 1):
        shapes += parts((3, 4))
    for _ in (0, 1):
        shapes += parts((3,))
    for _ in (0, 1):
        shapes += parts((4,))
    shapes += [pltpu.VMEM((HALF_ROWS[c], WIDTH[c]), F32) for c in range(5)]
    shapes += [
        pltpu.VMEM((3, T, D), BF),
        pltpu.VMEM((3, T, D), BF),
        pltpu.VMEM((D, T), BF),
        pltpu.VMEM((T, D), BF),
        pltpu.VMEM((T, D), F32),
        pltpu.VMEM((T, D), BF),
    ]
    shapes += [pltpu.VMEM(shape, kind) for shape, kind in KEPT]
    shapes += [
        pltpu.VMEM((TILE, 768), BF),
        pltpu.VMEM((TILE, 512), BF),
        pltpu.VMEM((TILE, 256), BF),
        pltpu.VMEM((T, D), BF),
    ]
    shapes += [
        pltpu.VMEM((8, D), F32),
        pltpu.VMEM((16, 128), F32),
        pltpu.VMEM((8, 512), F32),
        pltpu.VMEM((8, D), F32),
        pltpu.VMEM((8, 512), F32),
        pltpu.VMEM((T, 1), F32),
        pltpu.VMEM((6, TILE, TILE), F32),
        pltpu.VMEM((8, T), F32),
        pltpu.VMEM((8, T), F32),
    ]
    dma = pltpu.SemaphoreType.DMA
    shapes += [dma((2, 5, 11))] * 4 + [dma((5,)), dma((12,)), dma((2,)), dma((2,))]
    return shapes


KEPT = (
    ((3 * D, T), BF),
    ((HEADS, TILE, 768), BF),
    ((HEADS, TILE, 512), BF),
    ((HEADS, TILE, 256), BF),
    ((D, T), BF),
    ((HEADS, T), F32),
    ((T, FF), BF),
    ((T, FF), BF),
)


def body(
    inputs,
    cotangent,
    lengths,
    norm1_gain,
    norm1_bias,
    qkv_weight,
    qkv_bias,
    dense_weight,
    norm2_gain,
    norm2_bias,
    fc_in_weight,
    fc_in_bias,
    fc_out_weight,
    out_bias,
):
    z = lax.axis_index("shard") % 4
    here = (jnp.arange(4) == z).astype(F32)
    five = jnp.concatenate([norm1_gain, norm1_bias, norm2_gain, norm2_bias, out_bias], axis=0).astype(F32)
    five = (five[:, None, :] * here[None, :, None]).reshape(5, 128)
    three = (qkv_bias.astype(F32) * here[:, None]).reshape(3, 128)
    last = jnp.concatenate([three, fc_in_bias.astype(F32)], axis=0)
    vec = jnp.stack([jnp.pad(five, ((0, 3), (0, 0))), jnp.pad(last, ((0, 4), (0, 0)))])

    hbm = pl.BlockSpec(memory_space=pl.ANY)
    vmem = pl.BlockSpec(memory_space=pltpu.VMEM)
    shape = jax.ShapeDtypeStruct
    results = pl.pallas_call(
        kernel,
        out_shape=[shape((2, T, D), BF), shape((2, T, D), BF)]
        + [shape((2, HALF_ROWS[c], WIDTH[c]), F32) for c in range(5)]
        + [shape(s, k) for s, k in KEPT],
        in_specs=[pl.BlockSpec(memory_space=pltpu.SMEM)] + [hbm] * 7,
        out_specs=[hbm] * 2 + [vmem] * 5 + [hbm] * len(KEPT),
        scratch_shapes=scratch_shapes(),
        compiler_params=pltpu.CompilerParams(
            collective_id=0, has_side_effects=True, vmem_limit_bytes=64 * 1024 * 1024
        ),
        name="layers",
    )(lengths, inputs, cotangent, qkv_weight, dense_weight, fc_in_weight, fc_out_weight, vec)
    activations, input_grads, gq, gd, gi, go, gv = results[:7]
    five = jnp.sum(gv[0, :5].reshape(5, 4, 32) * here[None, :, None], axis=1)
    bias = jnp.sum(gv[1, :3].reshape(4, 96) * here[:, None], axis=0)[None]
    return (
        activations[None],
        input_grads[None],
        five[0:1],
        five[1:2],
        gq.reshape(1, 32, 1536),
        bias,
        gd.reshape(1, 32, 512),
        five[2:3],
        five[3:4],
        gi.reshape(1, 32, 2048),
        gv[1, 3:4],
        go.reshape(1, 128, 512),
        five[4:5],
    )


def solution(mesh):
    rows = P(None, ("replica", "shard"), None)
    vector, matrix = P("section", "shard"), P("section", "shard", None)
    slabs = P("section", None, ("replica", "shard"), None)
    return jax.shard_map(
        body,
        mesh=mesh,
        in_specs=(
            rows, rows, rows, vector, vector, matrix, vector, matrix, vector, vector, matrix, vector, matrix, vector,
        ),
        out_specs=(
            slabs, slabs, vector, vector, matrix, vector, matrix, vector, vector, matrix, vector, matrix, vector,
        ),
        check_vma=False,
    )
```

time: 1890 us -> 179 us (0.09)
  waiting for transfers between devices: 1050 us -> 0 us
  matrix products: 335 us -> 0 us
  Pallas kernels: 0 us -> 163 us
  blocking collectives: 159 us -> 0 us
  local copies, waits for them, and re-layouts: 151 us -> 11 us
  other arithmetic: 88.8 us -> 4 us
  loops' own time: 65.6 us -> 0 us
    reduce_scatter x12 -> x0, waiting for transfers between devices: 689 us -> none  [the longest x3 232 us: body(): lax.psum_scatter(grad_narrow_matrix.astype(jnp.bfloat16), 'shard', scatte...]
    dot_general x136 -> x0, matrix products: 335 us -> none  [the longest x32 52.2 us: one_head(): jnp.dot(head_query, head_key.T, preferred_element_type=jnp.float32)]
    ppermute x4 -> x0, waiting for transfers between devices: 272 us -> none  [passed_along(): lax.ppermute(value, axis, [(source, source + steps) for source in range(i...]
    pallas_call x0 -> x1, Pallas kernels: none -> 163 us  [body(): pl.pallas_call(kernel, out_shape=[shape((2, T, D), BF), shape((2, T, D),...]
    unnamed x1 -> x0, blocking collectives: 73 us -> none
    another operation x8 -> x0, loops' own time: 65.6 us -> none  [the longest x2 42 us: run_backward(): lax.map(one_head, jnp.arange(HEADS, dtype=jnp.int32))]
    psum x2 -> x0, waiting for transfers between devices: 46.3 us -> none  [the longest x1 42.8 us: body(): lax.psum(share_attend_matrix.astype(jnp.bfloat16), 'replica')]
    all_gather x2 -> x0, blocking collectives: 43.1 us -> none  [the longest x1 26.1 us: fetch_forward(): lax.all_gather(dense_weight, 'shard', axis=1, tiled=True)]
  transfers between devices with their start and end apart: 21 -> 0, of which waited for: 15 -> 0; matrix products, arithmetic and copies ran while one was open for 21% -> 0% of each run, Pallas kernels for 0% -> 0%
where the time goes in v1:
time: 179 us; the launch traced here: 178 us
  Pallas kernels  163 us (91%)
  local copies, waits for them, and re-layouts  11 us (6%)
  other arithmetic  4 us (2%)
    pallas_call x1, Pallas kernels, body(): pl.pallas_call(kernel, out_shape=[shape((2, T, D), BF), shape((2, T, D),...  163 us
    unnamed x18, local copies, waits for them, and re-layouts  6.65 us

profile of v1, /device:TPU:0, one launch (start us, length us, event | category | flops | bytes accessed | tf_op | source)
XLA Modules:
  0.0 178.4 jit_solution(3726046956207213293)
XLA Ops:
  0.7 0.0 copy-start.5
  0.7 0.7 bitcast_convert_fusion
  1.3 0.7 convert_element_type.28
  2.0 0.1 broadcast_multiply_fusion.1
  2.1 0.1 mul.75
  2.2 0.7 concatenate.10
  2.9 0.1 mul.66
  3.0 0.0 copy-done.5
  3.0 0.1 mul.67
  3.1 0.1 mul.65
  3.2 0.6 pad_maximum_fusion.vec_ref
  3.8 162.8 %layers.1 = (bf16[2,768,512]{2,1,0:T(8,128)(2,1)}, bf16[2,768,512]{2,1,0:T(8,128)(2,1)}, f32[2,16,1536]{2,1,0:T(8,128)}, f32[2,16,512]{2,1,0:T(8,128)}, f32[2,16...) custom-call(s32[2,1,4]{2,1,0:T(1,128)} %lengths.1, ...), custom_call_target="tpu_custom_call" | custom-call | tf_op jit(solution)/shard_map/layers/pallas_call | solution.py:944
  166.5 1.2 slice_bitcast_fusion
  167.7 0.7 slice.27
  168.4 0.7 slice.24
  169.1 0.1 reshape_squeeze.7
  169.2 1.2 multiply_reduce_fusion.1
  170.4 0.1 reshape_squeeze.6
  170.5 0.7 multiply_reduce_fusion
  171.3 0.5 fusion.1
  171.8 0.0 copy-start
  171.8 2.8 %copy.33 = bf16[1,2,768,512]{3,2,1,0:T(8,128)(2,1)} copy(bf16[1,2,768,512]{3,2,1,0:T(8,128)(2,1)} %bitcast.17) | data formatting | bytes 3145728
  174.6 0.0 copy-done
  174.6 0.0 copy-start.3
  174.6 0.0 copy-start.4
  174.6 0.0 copy-start.2
  174.6 0.0 copy-start.1
  174.6 1.1 copy.34
  175.7 0.0 copy-done.3
  175.7 0.7 copy.35
  176.4 0.0 copy-done.4
  176.4 0.6 copy.36
  177.0 0.0 copy-done.2
  177.0 0.7 copy.37
  177.7 0.0 copy-done.1
  177.7 0.7 copy.38
  (4 shorter events, 0.0 us)
Async XLA Ops:
  0.7 2.3 %copy-start.5 = (f32[4]{0:T(128)}, f32[4]{0:T(128)S(1)}, u32[]{:S(2)}) copy-start(f32[4]{0:T(128)S(1)} %compare_convert_fusion) | copy-start | bytes 52
  171.8 2.8 %copy-start = (bf16[2,768,512]{2,1,0:T(8,128)(2,1)S(1)}, bf16[2,768,512]{2,1,0:T(8,128)(2,1)}, u32[]{:S(2)}) copy-start(bf16[2,768,512]{2,1,0:T(8,128)(2,1)} %get-tuple-element.21) | copy-start | bytes 4718596
  174.6 1.2 copy-start.3
  174.6 1.8 %copy-start.4 = (f32[2,16,512]{2,1,0:T(8,128)S(1)}, f32[2,16,512]{2,1,0:T(8,128)}, u32[]{:S(2)}) copy-start(f32[2,16,512]{2,1,0:T(8,128)} %get-tuple-element.24) | copy-start | bytes 196612
  174.6 2.5 %copy-start.2 = (f32[2,16,2048]{2,1,0:T(8,128)S(1)}, f32[2,16,2048]{2,1,0:T(8,128)}, u32[]{:S(2)}) copy-start(f32[2,16,2048]{2,1,0:T(8,128)} %get-tuple-element.25) | copy-start | bytes 786436
  174.6 3.2 %copy-start.1 = (f32[2,64,512]{2,1,0:T(8,128)S(1)}, f32[2,64,512]{2,1,0:T(8,128)}, u32[]{:S(2)}) copy-start(f32[2,64,512]{2,1,0:T(8,128)} %get-tuple-element.26) | copy-start | bytes 786436
